TPU v7x, 32 devices: a whole 2x2x4 slice. The times are simulated.
32 devices in a mesh: grp: 2 (over core), gx: 4 (over y, x), gy: 4 (over z).
Axes of the slice: x: 2, y: 2, z: 4, core: 2. Of those that a mesh axis runs over, the one named last changes fastest.
Arguments:
- right_side: float32 [64, 64, 256], P('gx', 'gy', 'grp'), may hold values from -6 to 6
- coefficient: float32 [64, 64, 256], P('gx', 'gy', 'grp'), may hold values from 0.2 to 5
Outputs:
- solution_field: float32 [64, 64, 256], P('gx', 'gy', 'grp')
- residual: float32 [64, 64, 256], P('gx', 'gy', 'grp')
All inputs are finite; a program needn't handle non-finite values.
Results may differ from a plain program's by a relative error of at most 0.0001.
Values sent between devices are 32-bit elements; how exact they have to be, the bound alone decides.
A program may use at most 64 MiB of HBM per device.

v0:
```python
import jax
import jax.numpy as jnp
from jax import lax
from jax.sharding import PartitionSpec as P

FINE_DEGREE = 5
COARSE_DEGREE = 16
OUTER = 2


LOW_FINE = 0.2
LOW_COARSE = 0.02
HIGH_BOUND = 2.0
DAMPING = 0.5


def padded_2(block, sides, width):
    for axis, dim in sides:
        count = lax.axis_size(axis)
        forward = [(i, i + 1) for i in range(count - 1)]
        backward = [(target, source) for source, target in forward]
        low = lax.ppermute(
            lax.slice_in_dim(block, block.shape[dim] - width, None, axis=dim), axis, forward
        )
        high = lax.ppermute(lax.slice_in_dim(block, 0, width, axis=dim), axis, backward)
        block = jnp.concatenate([low, block, high], axis=dim)
    return block


def face_parts(padded):
    center = padded[1:-1, 1:-1, 1:-1]
    return (
        0.5 * (center + padded[:-2, 1:-1, 1:-1]),
        0.5 * (center + padded[2:, 1:-1, 1:-1]),
        0.5 * (center + padded[1:-1, :-2, 1:-1]),
        0.5 * (center + padded[1:-1, 2:, 1:-1]),
        0.5 * (center + padded[1:-1, 1:-1, :-2]),
        0.5 * (center + padded[1:-1, 1:-1, 2:]),
    )


def diagonal_of(parts):
    return parts[0] + parts[1] + parts[2] + parts[3] + parts[4] + parts[5]


def stencil(padded, parts, scale):
    center = padded[1:-1, 1:-1, 1:-1]
    nearby = parts[0] * padded[:-2, 1:-1, 1:-1] + parts[1] * padded[2:, 1:-1, 1:-1]
    nearby = nearby + parts[2] * padded[1:-1, :-2, 1:-1] + parts[3] * padded[1:-1, 2:, 1:-1]
    nearby = nearby + parts[4] * padded[1:-1, 1:-1, :-2] + parts[5] * padded[1:-1, 1:-1, 2:]
    return scale * (diagonal_of(parts) * center - nearby)


def restrict(field):
    size_a, size_b, size_c = field.shape
    return field.reshape(size_a // 2, 2, size_b // 2, 2, size_c // 2, 2).mean(axis=(1, 3, 5))


def prolong(field):
    return jnp.repeat(jnp.repeat(jnp.repeat(field, 2, 0), 2, 1), 2, 2)


def cheb_steps(degree, low, high):
    theta = (high + low) / 2.0
    delta = (high - low) / 2.0
    sigma = theta / delta
    rho = 1.0 / sigma
    keeps = []
    pushes = []
    for step in range(degree - 1):
        rho_new = 1.0 / (2.0 * sigma - rho)
        keeps.append(rho_new * rho)
        pushes.append(2.0 * rho_new / delta)
        rho = rho_new
    return (1.0 / theta, keeps, pushes)


def chebyshev(rhs, inverse_diag, apply_fn, degree, low, high):
    inv_theta, keeps, pushes = cheb_steps(degree, low, high)
    keep_table = jnp.array(keeps, jnp.float32)
    push_table = jnp.array(pushes, jnp.float32)
    first = inverse_diag * rhs * inv_theta

    def advance(step, carry):
        resid, update, total = carry
        resid = resid - apply_fn(update)
        update = keep_table[step] * update + push_table[step] * (inverse_diag * resid)
        return (resid, update, total + update)

    return lax.fori_loop(0, degree - 1, advance, (rhs, first, first))[2]


def field_halo(field):
    return padded_2(field, (("grp", 2), ("gx", 0), ("gy", 1)), 1)


def coef_faces(field):
    return face_parts(padded_2(field, (("grp", 2), ("gx", 0), ("gy", 1)), 1))


def collect(block):
    size_a, size_b, size_c = block.shape
    whole = lax.all_gather(block.reshape(-1), ("grp", "gx", "gy"), axis=0, tiled=True)
    whole = whole.reshape(
        lax.axis_size("grp"), lax.axis_size("gx"), lax.axis_size("gy"), size_a, size_b, size_c
    )
    whole = whole.transpose(1, 3, 2, 4, 0, 5)
    return whole.reshape(
        lax.axis_size("gx") * size_a, lax.axis_size("gy") * size_b, lax.axis_size("grp") * size_c
    )


def on_device(right_side, coefficient):
    scales = [1.0, 0.25, 0.0625, 0.015625]
    coefs = [coefficient]
    for level in range(3):
        coefs.append(restrict(coefs[-1]))
    parts_all = [coef_faces(coefs[level]) for level in range(3)]
    base_shape = coefs[3].shape
    whole_coef = collect(coefs[3])
    parts_all.append(face_parts(jnp.pad(whole_coef, 1)))
    inverses = [1.0 / (scales[level] * diagonal_of(parts_all[level])) for level in range(4)]

    def make_apply(level):
        return lambda field: stencil(field_halo(field), parts_all[level], scales[level])

    solution_field = jnp.zeros_like(right_side)
    residual = right_side
    for outer in range(OUTER):
        rhs_list = [residual]
        for level in range(3):
            rhs_list.append(restrict(rhs_list[-1]))
        corrections = [
            chebyshev(residual, inverses[0], make_apply(0), FINE_DEGREE, LOW_FINE, HIGH_BOUND)
        ]
        for level in range(1, 3):
            corrections.append(
                chebyshev(
                    rhs_list[level],
                    inverses[level],
                    make_apply(level),
                    FINE_DEGREE,
                    LOW_FINE,
                    HIGH_BOUND,
                )
            )
        whole_rhs = collect(rhs_list[3])
        whole_corr = chebyshev(
            whole_rhs,
            inverses[3],
            lambda field: stencil(jnp.pad(field, 1), parts_all[3], scales[3]),
            COARSE_DEGREE,
            LOW_COARSE,
            HIGH_BOUND,
        )
        corner = (
            lax.axis_index("gx") * base_shape[0],
            lax.axis_index("gy") * base_shape[1],
            lax.axis_index("grp") * base_shape[2],
        )
        corrections.append(lax.dynamic_slice(whole_corr, corner, base_shape))
        combined = corrections[2] + prolong(corrections[3])
        combined = corrections[1] + prolong(combined)
        combined = corrections[0] + prolong(combined)
        solution_field = solution_field + DAMPING * combined
        residual = right_side - stencil(field_halo(solution_field), parts_all[0], 1.0)
    return (solution_field, residual)


def solution(mesh):
    placed = (P("gx", "gy", "grp"), P("gx", "gy", "grp"))
    return jax.shard_map(
        on_device,
        mesh=mesh,
        in_specs=placed,
        out_specs=(P("gx", "gy", "grp"), P("gx", "gy", "grp")),
        check_vma=False,
    )
```

profile of v0, /device:TPU:0, one launch (start us, length us, event | category | flops | bytes accessed | tf_op | source)
XLA Modules:
  0.0 893.5 jit_solution(4941929132870313374)
XLA Ops:
  6.2 10.5 %reshape.122 = f32[8,2,8,2,64,2]{5,4,3,2,1,0:T(8,128)} reshape(f32[16,16,128]{2,1,0:T(8,128)} %param.35) | data formatting | bytes 262144 | tf_op jit(solution)/shard_map/reshape | solution.py:56
  24.8 9.8 %reshape.121 = f32[8,2,8,2,64,2]{5,4,3,2,1,0:T(8,128)} reshape(f32[16,16,128]{2,1,0:T(8,128)S(1)} %copy-done.2) | data formatting | bytes 262144 | tf_op jit(solution)/shard_map/reshape | solution.py:56
  81.2 40.6 %all-reduce.6 = (f32[2048]{0:T(1024)S(1)}, f32[2048]{0:T(1024)S(1)}) all-reduce(f32[2048]{0:T(1024)S(1)} %dynamic-update-slice, f32[2048]{0:T(1024)S(1)} %dynamic-update-slice.1), channel_id=1, replica_groups=mesh['grp'=2,'gx'=4,'gy'=4] {'grp','gx','gy'}, use_global_device_ids=true, to_apply=%add.3 | all-reduce | flops 4096 | bytes 32768
  122.6 36.3 %while.163 = (s32[]{:T(128)}, f32[8,8,32]{2,1,0:T(8,128)S(1)}, f32[8,8,32]{2,1,0:T(8,128)S(1)}, f32[8,8,32]{2,1,0:T(8,128)S(1)}, f32[8,8,32]{2,1,0:T(8,128)S(1)}...) while((s32[]{:T(128)}, f32[8,8,32]{2,1,0:T(8,128)S(1)}, ...), condition=%wide.region_13.14_spmd.clone, body=%wide.region_12.13_spmd.sunk.clone.sunk | while | flops 40962 | bytes 131253 | solution.py:90
  159.2 88.5 %while.162 = (s32[]{:T(128)}, f32[4,4,32]{2,1,0:T(4,128)S(1)}, f32[4,4,32]{2,1,0:T(4,128)S(1)}, f32[4,4,32]{2,1,0:T(4,128)S(1)}, f32[4,4,32]{2,1,0:T(4,128)S(1)}...) while((s32[]{:T(128)}, f32[4,4,32]{2,1,0:T(4,128)S(1)}, ...), condition=%wide.region_9.10_spmd.clone, body=%wide.region_8.9_spmd.sunk.clone.sunk | while | flops 21634 | bytes 55845 | solution.py:90
  209.4 5.7 collective-permute-start.15
  231.9 5.7 collective-permute-start.15
  254.5 91.0 %while.161 = (s32[]{:T(128)}, f32[8,8,64]{2,1,0:T(8,128)S(1)}, f32[8,8,64]{2,1,0:T(8,128)S(1)}, f32[8,8,64]{2,1,0:T(8,128)S(1)}, f32[8,8,64]{2,1,0:T(8,128)S(1)}...) while((s32[]{:T(128)}, f32[8,8,64]{2,1,0:T(8,128)S(1)}, ...), condition=%wide.region_5.6_spmd.clone, body=%wide.region_4.5_spmd.sunk.clone.sunk | while | flops 163042 | bytes 361189 | solution.py:90
  261.2 5.7 collective-permute-start.9
  306.9 5.7 collective-permute-start.9
  329.5 5.7 collective-permute-start.9
  347.0 93.3 %while.160 = (s32[]{:T(128)}, f32[16,16,128]{2,1,0:T(8,128)S(1)}, f32[16,16,128]{2,1,0:T(8,128)S(1)}, f32[16,16,128]{2,1,0:T(8,128)S(1)}, f32[16,16,128]{2,1,0:T...) while((s32[]{:T(128)}, f32[16,16,128]{2,1,0:T(8,128)S(1)}, ...), condition=%wide.region_1.0_spmd.clone, body=%wide.region_0.0_spmd.sunk.clone.sunk | while | flops 1239458 | bytes 2606949 | solution.py:90
  353.8 5.7 collective-permute-start.3
  377.1 5.7 collective-permute-start.3
  400.4 5.7 collective-permute-start.3
  423.8 5.7 collective-permute-start.3
  447.2 5.7 collective-permute-start.56
  462.4 9.8 %reshape.136 = f32[8,2,8,2,64,2]{5,4,3,2,1,0:T(8,128)} reshape(f32[16,16,128]{2,1,0:T(8,128)S(1)} %get-tuple-element.4128) | data formatting | bytes 262144 | tf_op jit(solution)/shard_map/reshape | solution.py:56
  478.2 44.7 %all-reduce.5 = f32[2048]{0:T(1024)S(1)} all-reduce(f32[2048]{0:T(1024)S(1)} %dynamic-update-slice.2), channel_id=1, replica_groups=mesh['grp'=2,'gx'=4,'gy'=4] {'grp','gx','gy'}, use_global_device_ids=true, to_apply=%add.5 | all-reduce | flops 2048 | bytes 16384
  523.3 59.2 %while.167 = (s32[]{:T(128)}, f32[8,8,32]{2,1,0:T(8,128)S(1)}, f32[8,8,32]{2,1,0:T(8,128)S(1)}, f32[8,8,32]{2,1,0:T(8,128)S(1)}, f32[8,8,32]{2,1,0:T(8,128)S(1)}...) while((s32[]{:T(128)}, f32[8,8,32]{2,1,0:T(8,128)S(1)}, ...), condition=%wide.region_24.25_spmd.clone, body=%wide.region_23.24_spmd.sunk.clone.sunk | while | flops 40962 | bytes 131253 | solution.py:90
  582.8 95.0 %while.166 = (s32[]{:T(128)}, f32[4,4,32]{2,1,0:T(4,128)S(1)}, f32[4,4,32]{2,1,0:T(4,128)S(1)}, f32[4,4,32]{2,1,0:T(4,128)S(1)}, f32[4,4,32]{2,1,0:T(4,128)S(1)}...) while((s32[]{:T(128)}, f32[4,4,32]{2,1,0:T(4,128)S(1)}, ...), condition=%wide.region_21.22_spmd.clone, body=%wide.region_20.21_spmd.sunk.clone.sunk | while | flops 21634 | bytes 55845 | solution.py:90
  636.3 5.7 collective-permute-start.33
  678.2 94.0 %while.165 = (s32[]{:T(128)}, f32[8,8,64]{2,1,0:T(8,128)S(1)}, f32[8,8,64]{2,1,0:T(8,128)S(1)}, f32[8,8,64]{2,1,0:T(8,128)S(1)}, f32[8,8,64]{2,1,0:T(8,128)S(1)}...) while((s32[]{:T(128)}, f32[8,8,64]{2,1,0:T(8,128)S(1)}, ...), condition=%wide.region_18.19_spmd.clone, body=%wide.region_17.18_spmd.sunk.clone.sunk | while | flops 163042 | bytes 361189 | solution.py:90
  708.3 5.7 collective-permute-start.27
  731.8 5.7 collective-permute-start.27
  755.3 5.7 collective-permute-start.27
  774.8 96.2 %while.164 = (s32[]{:T(128)}, f32[16,16,128]{2,1,0:T(8,128)S(1)}, f32[16,16,128]{2,1,0:T(8,128)S(1)}, f32[16,16,128]{2,1,0:T(8,128)S(1)}, f32[16,16,128]{2,1,0:T...) while((s32[]{:T(128)}, f32[16,16,128]{2,1,0:T(8,128)S(1)}, ...), condition=%wide.region_15.16_spmd.clone, body=%wide.region_14.15_spmd.sunk.clone.sunk | while | flops 1239458 | bytes 2606949 | solution.py:90
  781.6 5.7 collective-permute-start.21
  805.7 5.7 collective-permute-start.21
  829.7 5.7 collective-permute-start.21
  853.8 5.7 collective-permute-start.21
  877.9 5.7 collective-permute-start.62
  (789 shorter events, 664.5 us)
Async XLA Ops:
  1.7 59.1 %collective-permute-start.37 = (f32[16,16,1]{2,1,0:T(8,128)S(1)}, f32[16,16,1]{2,1,0:T(8,128)S(1)}, u32[]{:S(2)}, u32[]{:S(2)}) collective-permute-start(f32[16,16,1]{2,1,0:T(8,128)S(1)} %get-tuple-element.3222), channel_id=1, source_target_pairs={{16,0},{17,1},{18,2},{19,3},{20,4},{21,5},{22,6},{23,7},{24,8},{25... | collective-permute-start | bytes 3080 | tf_op jit(solution)/shard_map/ppermute | solution.py:25
  3.0 59.1 %collective-permute-start.36 = (f32[16,16,1]{2,1,0:T(8,128)S(1)}, f32[16,16,1]{2,1,0:T(8,128)S(1)}, u32[]{:S(2)}, u32[]{:S(2)}) collective-permute-start(f32[16,16,1]{2,1,0:T(8,128)S(1)} %get-tuple-element.3221), channel_id=1, source_target_pairs={{0,16},{1,17},{2,18},{3,19},{4,20},{5,21},{6,22},{7,23},{8,24},{9,... | collective-permute-start | bytes 3080 | tf_op jit(solution)/shard_map/ppermute | solution.py:22
  20.8 24.1 %collective-permute-start.43 = (f32[8,8,1]{2,1,0:T(8,128)S(1)}, f32[8,8,1]{2,1,0:T(8,128)S(1)}, u32[]{:S(2)}, u32[]{:S(2)}) collective-permute-start(f32[8,8,1]{2,1,0:T(8,128)S(1)} %get-tuple-element.3232), channel_id=1, source_target_pairs={{16,0},{17,1},{18,2},{19,3},{20,4},{21,5},{22,6},{23,7},{24,8},{25... | collective-permute-start | bytes 776 | tf_op jit(solution)/shard_map/ppermute | solution.py:25
  23.4 18.7 %collective-permute-start.49 = (f32[4,4,1]{2,1,0:T(4,128)S(1)}, f32[4,4,1]{2,1,0:T(4,128)S(1)}, u32[]{:S(2)}, u32[]{:S(2)}) collective-permute-start(f32[4,4,1]{2,1,0:T(4,128)S(1)} %get-tuple-element.3242), channel_id=1, source_target_pairs={{16,0},{17,1},{18,2},{19,3},{20,4},{21,5},{22,6},{23,7},{24,8},{25... | collective-permute-start | bytes 200 | tf_op jit(solution)/shard_map/ppermute | solution.py:25
  42.2 8.2 collective-permute-start.42
  43.6 8.2 collective-permute-start.51
  44.9 12.3 %collective-permute-start.50 = (f32[1,4,34]{2,1,0:T(4,128)S(1)}, f32[1,4,34]{2,1,0:T(4,128)S(1)}, u32[]{:S(2)}, u32[]{:S(2)}) collective-permute-start(f32[1,4,34]{2,1,0:T(4,128)S(1)} %get-tuple-element.3235), channel_id=1, source_target_pairs={{0,4},{4,8},{8,12},{1,5},{5,9},{9,13},{2,6},{6,10},{10,14},{3,7},{... | collective-permute-start | bytes 1640 | tf_op jit(solution)/shard_map/ppermute | solution.py:22
  50.4 13.1 %collective-permute-start.45 = (f32[1,8,66]{2,1,0:T(8,128)S(1)}, f32[1,8,66]{2,1,0:T(8,128)S(1)}, u32[]{:S(2)}, u32[]{:S(2)}) collective-permute-start(f32[1,8,66]{2,1,0:T(8,128)S(1)} %get-tuple-element.3226), channel_id=1, source_target_pairs={{4,0},{8,4},{12,8},{5,1},{9,5},{13,9},{6,2},{10,6},{14,10},{7,3},{... | collective-permute-start | bytes 6344 | tf_op jit(solution)/shard_map/ppermute | solution.py:25
  51.8 17.2 %collective-permute-start.44 = (f32[1,8,66]{2,1,0:T(8,128)S(1)}, f32[1,8,66]{2,1,0:T(8,128)S(1)}, u32[]{:S(2)}, u32[]{:S(2)}) collective-permute-start(f32[1,8,66]{2,1,0:T(8,128)S(1)} %get-tuple-element.3225), channel_id=1, source_target_pairs={{0,4},{4,8},{8,12},{1,5},{5,9},{9,13},{2,6},{6,10},{10,14},{3,7},{... | collective-permute-start | bytes 6344 | tf_op jit(solution)/shard_map/ppermute | solution.py:22
  57.3 16.3 %collective-permute-start.52 = (f32[6,1,34]{2,1,0:T(1,128)S(1)}, f32[6,1,34]{2,1,0:T(1,128)S(1)}, u32[]{:S(2)}, u32[]{:S(2)}) collective-permute-start(f32[6,1,34]{2,1,0:T(1,128)S(1)} %get-tuple-element.3234), channel_id=1, source_target_pairs={{0,1},{1,2},{2,3},{4,5},{5,6},{6,7},{8,9},{9,10},{10,11},{12,13},{... | collective-permute-start | bytes 2456 | tf_op jit(solution)/shard_map/ppermute | solution.py:22
  60.8 14.2 %collective-permute-start.53 = (f32[6,1,34]{2,1,0:T(1,128)S(1)}, f32[6,1,34]{2,1,0:T(1,128)S(1)}, u32[]{:S(2)}, u32[]{:S(2)}) collective-permute-start(f32[6,1,34]{2,1,0:T(1,128)S(1)} %get-tuple-element.3233), channel_id=1, source_target_pairs={{1,0},{2,1},{3,2},{5,4},{6,5},{7,6},{9,8},{10,9},{11,10},{13,12},{... | collective-permute-start | bytes 2456 | tf_op jit(solution)/shard_map/ppermute | solution.py:25
  62.2 186.5 %collective-permute-start.39 = (f32[1,16,130]{2,1,0:T(8,128)S(1)}, f32[1,16,130]{2,1,0:T(8,128)S(1)}, u32[]{:S(2)}, u32[]{:S(2)}) collective-permute-start(f32[1,16,130]{2,1,0:T(8,128)S(1)} %get-tuple-element.3216), channel_id=1, source_target_pairs={{4,0},{8,4},{12,8},{5,1},{9,5},{13,9},{6,2},{10,6},{14,10},{7,3},{... | collective-permute-start | bytes 24968 | tf_op jit(solution)/shard_map/ppermute | solution.py:25
  63.5 185.2 %collective-permute-start.38 = (f32[1,16,130]{2,1,0:T(8,128)S(1)}, f32[1,16,130]{2,1,0:T(8,128)S(1)}, u32[]{:S(2)}, u32[]{:S(2)}) collective-permute-start(f32[1,16,130]{2,1,0:T(8,128)S(1)} %get-tuple-element.3215), channel_id=1, source_target_pairs={{0,4},{4,8},{8,12},{1,5},{5,9},{9,13},{2,6},{6,10},{10,14},{3,7},{... | collective-permute-start | bytes 24968 | tf_op jit(solution)/shard_map/ppermute | solution.py:22
  248.9 97.6 %collective-permute-start.40 = (f32[18,1,130]{2,1,0:T(1,128)S(1)}, f32[18,1,130]{2,1,0:T(1,128)S(1)}, u32[]{:S(2)}, u32[]{:S(2)}) collective-permute-start(f32[18,1,130]{2,1,0:T(1,128)S(1)} %get-tuple-element.3210), channel_id=1, source_target_pairs={{0,1},{1,2},{2,3},{4,5},{5,6},{6,7},{8,9},{9,10},{10,11},{12,13},{... | collective-permute-start | bytes 28088 | tf_op jit(solution)/shard_map/ppermute | solution.py:22
  253.1 93.4 %collective-permute-start.41 = (f32[18,1,130]{2,1,0:T(1,128)S(1)}, f32[18,1,130]{2,1,0:T(1,128)S(1)}, u32[]{:S(2)}, u32[]{:S(2)}) collective-permute-start(f32[18,1,130]{2,1,0:T(1,128)S(1)} %get-tuple-element.3209), channel_id=1, source_target_pairs={{1,0},{2,1},{3,2},{5,4},{6,5},{7,6},{9,8},{10,9},{11,10},{13,12},{... | collective-permute-start | bytes 28088 | tf_op jit(solution)/shard_map/ppermute | solution.py:25
  268.3 7.7 collective-permute-start.10
  361.1 7.4 collective-permute-start.4
  384.4 7.4 collective-permute-start.4
  407.8 7.4 collective-permute-start.4
  431.1 7.4 collective-permute-start.4
  595.6 8.3 collective-permute-start.34
  619.4 8.3 collective-permute-start.34
  643.4 8.3 collective-permute-start.34
  667.5 8.3 collective-permute-start.34
  691.9 8.2 collective-permute-start.28
  715.4 8.2 collective-permute-start.28
  738.9 8.2 collective-permute-start.28
  762.4 8.2 collective-permute-start.28
  789.0 8.2 collective-permute-start.22
  813.0 8.2 collective-permute-start.22
  837.1 8.2 collective-permute-start.22
  861.1 8.2 collective-permute-start.22
  (170 other events, 2902.0 us)
where the time goes:
time: 903 us; the launch traced here: 894 us
  starting transfers between devices  495 us (55%)
  local copies, waits for them, and re-layouts  144 us (16%)
  other arithmetic  98 us (11%)
  blocking collectives  85.3 us (9%)
  waiting for transfers between devices  65.8 us (7%)
    ppermute x87, starting transfers between devices, padded_2(): lax.ppermute(lax.slice_in_dim(block, block.shape[dim] - width, None, axis...  383 us
    ppermute x87, starting transfers between devices, padded_2(): lax.ppermute(lax.slice_in_dim(block, 0, width, axis=dim), axis, backward)  112 us
    unnamed x2, blocking collectives  85.3 us
    add x54, other arithmetic, advance(): return (resid, update, total + update)  77 us
    ppermute x87, waiting for transfers between devices, padded_2(): lax.ppermute(lax.slice_in_dim(block, block.shape[dim] - width, None, axis...  61.5 us
    dynamic_slice x54, local copies, waits for them, and re-layouts, advance(): keep_table[step] * update + push_table[step] * (inverse_diag * resid)  50 us
    dynamic_slice x54, local copies, waits for them, and re-layouts, advance(): push_table[step] * (inverse_diag * resid)  49.8 us
    reshape x3, local copies, waits for them, and re-layouts, restrict(): field.reshape(size_a // 2, 2, size_b // 2, 2, size_c // 2, 2)  30.1 us
  transfers between devices with their start and end apart: 174, of which 63 were waited for; matrix products, arithmetic and copies ran while one was open for 14% of the time, Pallas kernels for 0%

commit v1 on v0

v1 whole, which is shorter than its diff:
```python
import functools

import jax
import jax.numpy as jnp
from jax import lax
from jax.experimental import pallas as pl
from jax.experimental.pallas import tpu as pltpu
from jax.sharding import PartitionSpec as P

FINE_DEGREE = 5
COARSE_DEGREE = 16
OUTER = 2
LOW_FINE = 0.2
LOW_COARSE = 0.02
HIGH_BOUND = 2.0
DAMPING = 0.5
H1 = 6
MESH = pl.DeviceIdType.MESH
F32 = jnp.float32


def cheb_steps(degree, low, high):
    theta = (high + low) / 2.0
    delta = (high - low) / 2.0
    sigma = theta / delta
    rho = 1.0 / sigma
    keeps = []
    pushes = []
    for step in range(degree - 1):
        rho_new = 1.0 / (2.0 * sigma - rho)
        keeps.append(rho_new * rho)
        pushes.append(2.0 * rho_new / delta)
        rho = rho_new
    return (1.0 / theta, keeps, pushes)


def dot(a, b):
    return jnp.dot(a, b, precision=lax.Precision.HIGHEST, preferred_element_type=F32)


def loop(low, high, body, unroll):
    whole = (high - low) // unroll
    if whole > 1:

        def several(i, carry):
            for j in range(unroll):
                body(low + i * unroll + j)
            return carry

        lax.fori_loop(0, whole, several, 0)
    else:
        whole = 0
    for p in range(low + whole * unroll, high):
        body(p)


def pick(rows, columns, rule, value=1.0):
    i = lax.broadcasted_iota(jnp.int32, (rows, columns), 0)
    j = lax.broadcasted_iota(jnp.int32, (rows, columns), 1)
    return jnp.where(rule(i, j), value, 0.0).astype(F32)


def build(a, w, inv, low, high, unroll, diag=None):
    rows, lanes = a.shape[-2:]
    i = lax.broadcasted_iota(jnp.int32, (rows, lanes), 0)
    j = lax.broadcasted_iota(jnp.int32, (rows, lanes), 1)

    def body(p):
        c = a[p]
        near = (
            a[p - 1],
            a[p + 1],
            jnp.where(i == 0, 0.0, pltpu.roll(c, 1, 0)),
            jnp.where(i == rows - 1, 0.0, pltpu.roll(c, rows - 1, 0)),
            jnp.where(j == 0, 0.0, pltpu.roll(c, 1, 1)),
            jnp.where(j == lanes - 1, 0.0, pltpu.roll(c, lanes - 1, 1)),
        )
        faces = [0.5 * (c + n) for n in near]
        total = faces[0] + faces[1] + faces[2] + faces[3] + faces[4] + faces[5]
        good = c > 0.0
        inverse = jnp.where(good, 1.0 / jnp.where(good, total, 1.0), 0.0)
        inv[p] = inverse
        if diag is not None:
            diag[p] = total
        for k in range(6):
            w[k, p] = jnp.where(near[k] > 0.0, faces[k] * inverse, 0.0)

    loop(low, high, body, unroll)


def nearby(w, v, p):
    c = v[p]
    rows, lanes = c.shape
    acc = w[0, p] * v[p - 1] + w[1, p] * v[p + 1]
    acc2 = w[2, p] * pltpu.roll(c, 1, 0) + w[3, p] * pltpu.roll(c, rows - 1, 0)
    acc3 = w[4, p] * pltpu.roll(c, 1, 1) + w[5, p] * pltpu.roll(c, lanes - 1, 1)
    return c, acc + (acc2 + acc3)


def first_update(r, inv, t, d, scale, inv_theta, low, high, unroll):
    def body(p):
        start = r[p] * inv[p] * (1.0 / scale)
        t[p] = start
        d[p] = start * inv_theta

    loop(low, high, body, unroll)


def advance(w, t, d, d_next, keep, push, low, high, unroll, total=None):
    def body(p):
        c, acc = nearby(w, d, p)
        left = t[p] - c + acc
        t[p] = left
        new = keep * c + push * left
        d_next[p] = new
        if total is not None:
            total[p] = total[p] + new

    loop(low, high, body, unroll)


def kernel(
    gx_size, gy_size,
    rhs_ref, coef_ref, sol_ref, res_ref,
    f1, w1, inv1, diag1, t1, d1, u1, last,
    f2, w2, inv2, t2, d2, c2,
    gath, f3, w3, inv3, t3, d3, c3,
    f4, w4, inv4, t4, d4, c4,
    pair_send, pair_recv, s1_send, s1_recv, s2_send, s2_recv, gy_send, gy_recv, gx_send, gx_recv,
    out_send, out_recv,
):
    g = lax.axis_index("grp")
    gy = lax.axis_index("gy")
    nx = 2 * gx_size
    xi = 2 * lax.axis_index("gx") + g
    full_x, by, half_z = rhs_ref.shape
    bx = full_x // 2
    lanes1 = 2 * half_z
    lanes = half_z
    y2, y3, y4 = by // 2, f3.shape[2], f4.shape[2]
    b2 = bx // 2
    n3, n4 = f3.shape[1] - 2, f4.shape[1] - 2

    def where_is(x, y):
        return {"grp": lax.rem(x, 2), "gx": lax.div(x, 2), "gy": y}

    def valid(dx, dy):
        x, y = xi + dx, gy + dy
        return (x >= 0) & (x < nx) & (y >= 0) & (y < gy_size)

    def remote(src, dst, send, recv, x, y):
        return pltpu.make_async_remote_copy(
            src_ref=src, dst_ref=dst, send_sem=send, recv_sem=recv,
            device_id=where_is(x, y), device_id_type=MESH,
        )

    def clear1(p):
        for q in range(3):
            f1[q, p] = jnp.zeros(f1.shape[2:], F32)

    loop(0, f1.shape[1], clear1, 1)

    def clear2(p):
        for q in range(3):
            f2[q, p] = jnp.zeros(f2.shape[2:], F32)

    loop(0, f2.shape[1], clear2, 2)
    for q in (0, 1):
        for p in (0, n3 + 1):
            f3[q, p] = jnp.zeros(f3.shape[2:], F32)
        for p in (0, n4 + 1):
            f4[q, p] = jnp.zeros(f4.shape[2:], F32)
    for k in range(FINE_DEGREE):
        for p in (0, n3 + 1):
            d3[k, p] = jnp.zeros(d3.shape[2:], F32)
    for k in range(2):
        for p in (0, n4 + 1):
            d4[k, p] = jnp.zeros(d4.shape[2:], F32)

    around = [(dx, dy) for dx in range(-2, 3) for dy in range(-1, 2) if (dx, dy) != (0, 0)]
    close = [(dx, dy) for dx, dy in around if abs(dx) < 2]

    barrier = pltpu.get_barrier_semaphore()
    for dx, dy in around:

        @pl.when(valid(dx, dy))
        def _(dx=dx, dy=dy):
            pl.semaphore_signal(barrier, 1, device_id=where_is(xi + dx, gy + dy), device_id_type=MESH)

    for o in range(1, gy_size):
        pl.semaphore_signal(barrier, 1, device_id=where_is(xi, lax.rem(gy + o, gy_size)), device_id_type=MESH)
    for o in range(1, nx):
        pl.semaphore_signal(barrier, 1, device_id=where_is(lax.rem(xi + o, nx), gy), device_id_type=MESH)
    count_x = 1 + sum(jnp.where((xi + dx >= 0) & (xi + dx < nx), 1, 0) for dx in (-2, -1, 1, 2))
    count_y = 1 + sum(jnp.where((gy + dy >= 0) & (gy + dy < gy_size), 1, 0) for dy in (-1, 1))
    pl.semaphore_wait(barrier, count_x * count_y - 1 + gy_size - 1 + nx - 1)

    own_x = pl.ds(H1, bx)
    own_y = pl.ds(8, by)
    mine_z = pl.ds(pl.multiple_of(g * half_z, half_z), half_z)
    their_z = pl.ds(pl.multiple_of((1 - g) * half_z, half_z), half_z)
    mine_x = pl.ds(g * bx, bx)
    their_x = pl.ds((1 - g) * bx, bx)
    partner = xi + 1 - 2 * g
    swaps = [
        remote(ref.at[their_x], f1.at[q, own_x, own_y, mine_z], pair_send.at[q], pair_recv.at[q], partner, gy)
        for q, ref in ((0, coef_ref), (1, rhs_ref))
    ]
    for copy in swaps:
        copy.start()
    for q, ref in ((0, coef_ref), (1, rhs_ref)):
        f1[q, own_x, own_y, mine_z] = ref[mine_x]
    arrivals = [
        remote(ref.at[their_x], f1.at[q, own_x, own_y, their_z], pair_send.at[q], pair_recv.at[q], partner, gy)
        for q, ref in ((0, coef_ref), (1, rhs_ref))
    ]
    for copy in swaps:
        copy.wait_send()
    for copy in arrivals:
        copy.wait_recv()

    half_z_mat = pick(lanes1, lanes, lambda i, j: (i >> 1) == j, 0.125)
    half_y_mat = pick(y2, by, lambda i, j: (j >> 1) == i)
    half_z2 = pick(lanes, lanes, lambda i, j: (i >> 1) == j, 0.125)
    quarter_y = [pick(8, y2, lambda i, j, r=r: i == r * (by // 4) + (j >> 1)) for r in range(bx // 4)]
    half_y3 = pick(y4, y3, lambda i, j: (j >> 1) == i)
    twice_z = pick(lanes, lanes, lambda i, j: (j >> 1) == i)
    twice_z1 = pick(lanes, lanes1, lambda i, j: (j >> 1) == i)
    twice_y3 = pick(y3, y4, lambda i, j: (i >> 1) == j)
    twice_y2 = pick(f2.shape[2], y3, lambda i, j: ((gy * y2 - 8 + i) >> 1) == j)
    twice_y1 = pick(f1.shape[2], f2.shape[2], lambda i, j: (i >> 1) + 4 == j)
    spread = [
        pick(y3, gy_size * 8, lambda i, j, r=r: j == (i >> 2) * 8 + r * (by // 4) + (i & 3)) for r in range(bx // 4)
    ]

    fine = cheb_steps(FINE_DEGREE, LOW_FINE, HIGH_BOUND)
    coarse = cheb_steps(COARSE_DEGREE, LOW_COARSE, HIGH_BOUND)

    for outer in range(OUTER):
        q0, count = ((0, 2), (2, 1))[outer]
        qs = pl.ds(q0, count)
        now = q0 + count - 1

        copies1 = []
        for k, (dx, dy) in enumerate(close):
            src_x, dst_x = {
                0: (own_x, own_x),
                1: (pl.ds(bx, H1), pl.ds(0, H1)),
                -1: (pl.ds(H1, H1), pl.ds(H1 + bx, H1)),
            }[dx]
            src_y, dst_y = {
                0: (own_y, own_y),
                1: (pl.ds(by, 8), pl.ds(0, 8)),
                -1: (pl.ds(8, 8), pl.ds(8 + by, 8)),
            }[dy]
            copies1.append((dx, dy, remote(
                f1.at[qs, src_x, src_y], f1.at[qs, dst_x, dst_y],
                s1_send.at[outer, k], s1_recv.at[outer, k], xi + dx, gy + dy,
            )))
        copies2 = []
        for k, (dx, dy) in enumerate(around):
            copies2.append((dx, dy, remote(
                f2.at[qs, pl.ds(2 * b2, b2), pl.ds(8, y2)],
                f2.at[qs, pl.ds(2 * b2 - b2 * dx, b2), pl.ds(8 - y2 * dy, y2)],
                s2_send.at[outer, k], s2_recv.at[outer, k], xi + dx, gy + dy,
            )))

        def start(copies):
            for dx, dy, copy in copies:
                pl.when(valid(dx, dy))(copy.start)

        def finish(copies):
            for dx, dy, copy in copies:
                pl.when(valid(-dx, -dy))(copy.wait_recv)

        def drain(copies):
            for dx, dy, copy in copies:
                pl.when(valid(dx, dy))(copy.wait_send)

        start(copies1)
        for q in range(q0, q0 + count):
            for p in range(b2):
                both = f1[q, H1 + 2 * p, 8 : 8 + by] + f1[q, H1 + 2 * p + 1, 8 : 8 + by]
                f2[q, 2 * b2 + p, 8 : 8 + y2] = dot(half_y_mat, dot(both, half_z_mat))
        start(copies2)
        for q in range(q0, q0 + count):
            tile = jnp.zeros((8, lanes), F32)
            for r in range(bx // 4):
                both = f2[q, 2 * b2 + 2 * r, 8 : 8 + y2] + f2[q, 2 * b2 + 2 * r + 1, 8 : 8 + y2]
                tile = tile + dot(quarter_y[r], dot(both, half_z2))
            gath[q, xi, gy] = tile

        def along_y(o):
            return remote(
                gath.at[qs, xi, gy], gath.at[qs, xi, gy],
                gy_send.at[outer, o], gy_recv.at[outer, o], xi, lax.rem(gy + o, gy_size),
            )

        def from_y(o):
            y = lax.rem(gy + gy_size - o, gy_size)
            return remote(
                gath.at[qs, xi, y], gath.at[qs, xi, y],
                gy_send.at[outer, o], gy_recv.at[outer, o], xi, lax.rem(gy + o, gy_size),
            )

        def along_x(o):
            return remote(
                gath.at[qs, xi], gath.at[qs, xi],
                gx_send.at[outer, o], gx_recv.at[outer, o], lax.rem(xi + o, nx), gy,
            )

        def from_x(o):
            x = lax.rem(xi + nx - o, nx)
            return remote(
                gath.at[qs, x], gath.at[qs, x],
                gx_send.at[outer, o], gx_recv.at[outer, o], lax.rem(xi + o, nx), gy,
            )

        for o in range(1, gy_size):
            along_y(o).start()
        for o in range(1, gy_size):
            from_y(o).wait_recv()
        for o in range(1, nx):
            along_x(o).start()

        finish(copies2)
        low, high = 2 * b2 - 5, 3 * b2 + 5
        if outer == 0:
            build(f2.at[0], w2, inv2, low, high, 2)
        first_update(f2.at[now], inv2, t2, d2.at[0], 0.25, fine[0], low, high, 7)
        for k in range(FINE_DEGREE - 1):
            low, high = low + 1, high - 1
            advance(w2, t2, d2.at[k], d2.at[k + 1], fine[1][k], fine[2][k], low, high, 4)
        low2 = low

        for o in range(1, nx):
            from_x(o).wait_recv()
        for q in range(q0, q0 + count):
            slot = 0 if q == 0 else 1

            def unpack(x, q=q, slot=slot):
                tiles = gath[q, x].reshape(gy_size * 8, lanes)
                for r in range(bx // 4):
                    f3[slot, 1 + x * (bx // 4) + r] = dot(spread[r], tiles)

            loop(0, nx, unpack, 4)

            def shrink(x, slot=slot):
                both = f3[slot, 1 + 2 * x] + f3[slot, 2 + 2 * x]
                f4[slot, 1 + x] = dot(half_y3, dot(both, half_z2))

            loop(0, n4, shrink, 4)
        if outer == 0:
            build(f3.at[0], w3, inv3, 1, n3 + 1, 4)
            build(f4.at[0], w4, inv4, 1, n4 + 1, 4)
        first_update(f4.at[1], inv4, t4, d4.at[0], 0.015625, coarse[0], 1, n4 + 1, 8)

        def begin4(p):
            c4[p] = d4[0, p]

        loop(1, n4 + 1, begin4, 8)
        for k in range(COARSE_DEGREE - 1):
            advance(w4, t4, d4.at[k % 2], d4.at[(k + 1) % 2], coarse[1][k], coarse[2][k], 1, n4 + 1, 8, c4)
        first_update(f3.at[1], inv3, t3, d3.at[0], 0.0625, fine[0], 1, n3 + 1, 8)
        for k in range(FINE_DEGREE - 1):
            advance(w3, t3, d3.at[k], d3.at[k + 1], fine[1][k], fine[2][k], 1, n3 + 1, 4)

        def combine3(x):
            wide = dot(twice_y3, dot(c4[1 + x], twice_z))
            for p in (1 + 2 * x, 2 + 2 * x):
                c3[p] = ((d3[0, p] + d3[1, p]) + (d3[2, p] + d3[3, p])) + d3[4, p] + wide

        loop(0, n4, combine3, 4)
        b3 = b2 // 2
        for r in range(-1, b3 + 1):
            plane = jnp.clip(xi * b3 + r, 0, n3 - 1) + 1
            wide = dot(twice_y2, dot(c3[plane], twice_z))
            for p in (2 * b2 + 2 * r, 2 * b2 + 2 * r + 1):
                if 2 * b2 - 1 <= p < 3 * b2 + 1:
                    c2[p] = ((d2[0, p] + d2[1, p]) + (d2[2, p] + d2[3, p])) + d2[4, p] + wide

        finish(copies1)
        low, high = H1 - 5, H1 + bx + 5
        if outer == 0:
            build(f1.at[0], w1, inv1, low, high, 1, diag1)
        first_update(f1.at[now], inv1, t1, d1.at[0], 1.0, fine[0], low, high, 2)
        for k in range(FINE_DEGREE - 1):
            low, high = low + 1, high - 1
            advance(w1, t1, d1.at[k], d1.at[k + 1], fine[1][k], fine[2][k], low, high, 2)

        def combine1(r):
            wide = dot(twice_y1, dot(c2[2 * b2 + r], twice_z1))
            return wide

        for r in range(-1, b2 + 1):
            wide = combine1(r)
            for p in (H1 + 2 * r, H1 + 2 * r + 1):
                if H1 - 1 <= p < H1 + bx + 1:
                    both = ((d1[0, p] + d1[1, p]) + (d1[2, p] + d1[3, p])) + d1[4, p] + wide
                    if outer == 0:
                        u1[p] = DAMPING * both
                    else:
                        u1[p] = u1[p] + DAMPING * both

        def leftover(p):
            c, acc = nearby(w1, u1, p)
            value = f1[1, p] - diag1[p] * (c - acc)
            if outer + 1 < OUTER:
                f1[2, p, 8 : 8 + by] = value[8 : 8 + by]
            else:
                last[p - H1] = value[8 : 8 + by]

        loop(H1, H1 + bx, leftover, 2)
        drain(copies1)
        drain(copies2)
        for o in range(1, gy_size):
            along_y(o).wait_send()
        for o in range(1, nx):
            along_x(o).wait_send()

    outs = [
        remote(u1.at[own_x, own_y, their_z], sol_ref.at[mine_x], out_send.at[0], out_recv.at[0], partner, gy),
        remote(last.at[:, :, their_z], res_ref.at[mine_x], out_send.at[1], out_recv.at[1], partner, gy),
    ]
    for copy in outs:
        copy.start()
    sol_ref[mine_x] = u1[own_x, own_y, mine_z]
    res_ref[mine_x] = last[:, :, mine_z]
    for copy in outs:
        copy.wait_send()
    remote(u1.at[own_x, own_y, their_z], sol_ref.at[their_x], out_send.at[0], out_recv.at[0], partner, gy).wait_recv()
    remote(last.at[:, :, their_z], res_ref.at[their_x], out_send.at[1], out_recv.at[1], partner, gy).wait_recv()


def solution(mesh):
    gx_size, gy_size = mesh.shape["gx"], mesh.shape["gy"]

    def on_device(right_side, coefficient):
        full_x, by, half_z = right_side.shape
        bx = full_x // 2
        nx = 2 * gx_size
        lanes = half_z
        p1, r1, l1 = bx + 2 * H1, by + 16, 2 * half_z
        b2, y2 = bx // 2, by // 2
        p2, r2 = 5 * b2, y2 + 16
        p3, r3 = nx * bx // 4 + 2, gy_size * by // 4
        p4, r4 = nx * bx // 8 + 2, gy_size * by // 8
        vm = lambda *shape: pltpu.VMEM(shape, F32)
        sem = lambda *shape: pltpu.SemaphoreType.DMA(shape)
        return pl.pallas_call(
            functools.partial(kernel, gx_size, gy_size),
            out_shape=(jax.ShapeDtypeStruct(right_side.shape, F32),) * 2,
            in_specs=[pl.BlockSpec(memory_space=pltpu.VMEM)] * 2,
            out_specs=(pl.BlockSpec(memory_space=pltpu.VMEM),) * 2,
            scratch_shapes=[
                vm(3, p1, r1, l1), vm(6, p1, r1, l1), vm(p1, r1, l1), vm(p1, r1, l1), vm(p1, r1, l1),
                vm(FINE_DEGREE, p1, r1, l1), vm(p1, r1, l1), vm(bx, by, l1),
                vm(3, p2, r2, lanes), vm(6, p2, r2, lanes), vm(p2, r2, lanes), vm(p2, r2, lanes),
                vm(FINE_DEGREE, p2, r2, lanes), vm(p2, r2, lanes),
                vm(3, nx, gy_size, 8, lanes),
                vm(2, p3, r3, lanes), vm(6, p3, r3, lanes), vm(p3, r3, lanes), vm(p3, r3, lanes),
                vm(FINE_DEGREE, p3, r3, lanes), vm(p3, r3, lanes),
                vm(2, p4, r4, lanes), vm(6, p4, r4, lanes), vm(p4, r4, lanes), vm(p4, r4, lanes),
                vm(2, p4, r4, lanes), vm(p4, r4, lanes),
                sem(2), sem(2), sem(2, 8), sem(2, 8), sem(2, 14), sem(2, 14),
                sem(2, gy_size), sem(2, gy_size), sem(2, nx), sem(2, nx), sem(2), sem(2),
            ],
            compiler_params=pltpu.CompilerParams(
                collective_id=0, has_side_effects=True, vmem_limit_bytes=48 * 1024 * 1024
            ),
        )(right_side, coefficient)

    placed = (P("gx", "gy", "grp"), P("gx", "gy", "grp"))
    return jax.shard_map(on_device, mesh=mesh, in_specs=placed, out_specs=placed, check_vma=False)
```

time: 903 us -> 76.3 us (0.08); the launches traced: 894 us -> 76.2 us
  starting transfers between devices: 495 us -> 0 us
  local copies, waits for them, and re-layouts: 144 us -> 3.11 us
  other arithmetic: 98 us -> 0 us
  blocking collectives: 85.3 us -> 0 us
  Pallas kernels: 0 us -> 72.4 us
  waiting for transfers between devices: 65.8 us -> 0 us
    ppermute x174 -> x0, starting transfers between devices: 495 us -> none  [the longest x87 383 us: padded_2(): lax.ppermute(lax.slice_in_dim(block, block.shape[dim] - width, None, axis...]
    dynamic_slice x110 -> x0, local copies, waits for them, and re-layouts: 100 us -> none  [the longest x54 50 us: advance(): keep_table[step] * update + push_table[step] * (inverse_diag * resid)]
    unnamed x2 -> x0, blocking collectives: 85.3 us -> none
    add x60 -> x0, other arithmetic: 77.4 us -> none  [the longest x54 77 us: advance(): return (resid, update, total + update)]
    pallas_call x0 -> x1, Pallas kernels: none -> 72.4 us  [on_device(): pl.pallas_call(functools.partial(kernel, gx_size, gy_size), out_shape=(ja...]
    ppermute x174 -> x0, waiting for transfers between devices: 65.8 us -> none  [the longest x87 61.5 us: padded_2(): lax.ppermute(lax.slice_in_dim(block, block.shape[dim] - width, None, axis...]
    reshape x21 -> x0, local copies, waits for them, and re-layouts: 33.8 us -> none  [the longest x3 30.1 us: restrict(): field.reshape(size_a // 2, 2, size_b // 2, 2, size_c // 2, 2)]
    reduce_sum x9 -> x0, other arithmetic: 12.9 us -> none  [restrict(): field.reshape(size_a // 2, 2, size_b // 2, 2, size_c // 2, 2)]
  transfers between devices with their start and end apart: 174 -> 0, of which waited for: 63 -> 0; matrix products, arithmetic and copies ran while one was open for 14% -> 0% of each run, Pallas kernels for 0% -> 0%
where the time goes in v1:
time: 76.3 us; the launch traced here: 76.2 us
  Pallas kernels  72.4 us (95%)
  local copies, waits for them, and re-layouts  3.11 us (4%)
    pallas_call x1, Pallas kernels, on_device(): pl.pallas_call(functools.partial(kernel, gx_size, gy_size), out_shape=(ja...  72.4 us
    unnamed x6, local copies, waits for them, and re-layouts  3.11 us

profile of v1, /device:TPU:0, one launch (start us, length us, event | category | flops | bytes accessed | tf_op | source)
XLA Modules:
  0.0 76.2 jit_solution(9384739479414148100)
XLA Ops:
  0.6 0.0 copy-start
  0.6 0.9 %copy-done = f32[16,16,128]{2,1,0:T(8,128)S(1)} copy-done((f32[16,16,128]{2,1,0:T(8,128)S(1)}, f32[16,16,128]{2,1,0:T(8,128)}, u32[]{:S(2)}) %copy-start) | copy-done | bytes 131096
  1.5 0.0 copy-start.1
  1.5 0.9 %copy-done.1 = f32[16,16,128]{2,1,0:T(8,128)S(1)} copy-done((f32[16,16,128]{2,1,0:T(8,128)S(1)}, f32[16,16,128]{2,1,0:T(8,128)}, u32[]{:S(2)}) %copy-start.1) | copy-done | bytes 131096
  2.4 72.4 %shard_map.41 = (f32[16,16,128]{2,1,0:T(8,128)S(1)}, f32[16,16,128]{2,1,0:T(8,128)S(1)}) custom-call(f32[16,16,128]{2,1,0:T(8,128)S(1)} %copy-done, f32[16,16,128]{2,1,0:T(8,128)S(1)} %copy-done.1), custom_call_target="tpu_custom_call" | custom-call | tf_op jit(solution)/shard_map/pallas_call | solution.py:450
  74.9 0.7 copy.6
  75.5 0.7 copy.7
Async XLA Ops:
  0.6 0.9 %copy-start = (f32[16,16,128]{2,1,0:T(8,128)S(1)}, f32[16,16,128]{2,1,0:T(8,128)}, u32[]{:S(2)}) copy-start(f32[16,16,128]{2,1,0:T(8,128)} %rhs_ref.1) | copy-start | bytes 393220
  1.5 0.9 %copy-start.1 = (f32[16,16,128]{2,1,0:T(8,128)S(1)}, f32[16,16,128]{2,1,0:T(8,128)}, u32[]{:S(2)}) copy-start(f32[16,16,128]{2,1,0:T(8,128)} %coef_ref.1) | copy-start | bytes 393220

commit v2 on v1

--- a/solution.py
+++ b/solution.py
@@ -126,6 +126,7 @@
     f2, w2, inv2, t2, d2, c2,
     gath, f3, w3, inv3, t3, d3, c3,
     f4, w4, inv4, t4, d4, c4,
+    tmp, c1, load_sem,
     pair_send, pair_recv, s1_send, s1_recv, s2_send, s2_recv, gy_send, gy_recv, gx_send, gx_recv,
     out_send, out_recv,
 ):
@@ -165,6 +166,19 @@
             f2[q, p] = jnp.zeros(f2.shape[2:], F32)
 
     loop(0, f2.shape[1], clear2, 2)
+    own_x = pl.ds(H1, bx)
+    own_y = pl.ds(8, by)
+    mine_z = pl.ds(pl.multiple_of(g * half_z, half_z), half_z)
+    their_z = pl.ds(pl.multiple_of((1 - g) * half_z, half_z), half_z)
+    mine_x = pl.ds(g * bx, bx)
+    their_x = pl.ds((1 - g) * bx, bx)
+    partner = xi + 1 - 2 * g
+    loads = [
+        pltpu.make_async_copy(ref.at[mine_x], f1.at[q, own_x, own_y, mine_z], load_sem.at[q])
+        for q, ref in ((0, coef_ref), (1, rhs_ref))
+    ]
+    for copy in loads:
+        copy.start()
     for q in (0, 1):
         for p in (0, n3 + 1):
             f3[q, p] = jnp.zeros(f3.shape[2:], F32)
@@ -195,21 +209,12 @@
     count_y = 1 + sum(jnp.where((gy + dy >= 0) & (gy + dy < gy_size), 1, 0) for dy in (-1, 1))
     pl.semaphore_wait(barrier, count_x * count_y - 1 + gy_size - 1 + nx - 1)
 
-    own_x = pl.ds(H1, bx)
-    own_y = pl.ds(8, by)
-    mine_z = pl.ds(pl.multiple_of(g * half_z, half_z), half_z)
-    their_z = pl.ds(pl.multiple_of((1 - g) * half_z, half_z), half_z)
-    mine_x = pl.ds(g * bx, bx)
-    their_x = pl.ds((1 - g) * bx, bx)
-    partner = xi + 1 - 2 * g
     swaps = [
         remote(ref.at[their_x], f1.at[q, own_x, own_y, mine_z], pair_send.at[q], pair_recv.at[q], partner, gy)
         for q, ref in ((0, coef_ref), (1, rhs_ref))
     ]
     for copy in swaps:
         copy.start()
-    for q, ref in ((0, coef_ref), (1, rhs_ref)):
-        f1[q, own_x, own_y, mine_z] = ref[mine_x]
     arrivals = [
         remote(ref.at[their_x], f1.at[q, own_x, own_y, their_z], pair_send.at[q], pair_recv.at[q], partner, gy)
         for q, ref in ((0, coef_ref), (1, rhs_ref))
@@ -218,20 +223,34 @@
         copy.wait_send()
     for copy in arrivals:
         copy.wait_recv()
+    for copy in loads:
+        copy.wait()
 
     half_z_mat = pick(lanes1, lanes, lambda i, j: (i >> 1) == j, 0.125)
-    half_y_mat = pick(y2, by, lambda i, j: (j >> 1) == i)
     half_z2 = pick(lanes, lanes, lambda i, j: (i >> 1) == j, 0.125)
-    quarter_y = [pick(8, y2, lambda i, j, r=r: i == r * (by // 4) + (j >> 1)) for r in range(bx // 4)]
-    half_y3 = pick(y4, y3, lambda i, j: (j >> 1) == i)
     twice_z = pick(lanes, lanes, lambda i, j: (j >> 1) == i)
     twice_z1 = pick(lanes, lanes1, lambda i, j: (j >> 1) == i)
-    twice_y3 = pick(y3, y4, lambda i, j: (i >> 1) == j)
-    twice_y2 = pick(f2.shape[2], y3, lambda i, j: ((gy * y2 - 8 + i) >> 1) == j)
-    twice_y1 = pick(f1.shape[2], f2.shape[2], lambda i, j: (i >> 1) + 4 == j)
-    spread = [
-        pick(y3, gy_size * 8, lambda i, j, r=r: j == (i >> 2) * 8 + r * (by // 4) + (i & 3)) for r in range(bx // 4)
-    ]
+    rows1, rows2 = f1.shape[2], f2.shape[2]
+    b3 = b2 // 2
+
+    def blocks(count, rows, columns, rule):
+        def whole(i, j):
+            found = False
+            for r in range(count):
+                a, b = i - r * rows, j - r * columns
+                found = found | ((a >= 0) & (a < rows) & (b >= 0) & (b < columns) & rule(a, b))
+            return found
+
+        return pick(count * rows, count * columns, whole)
+
+    twice_y2 = blocks(b3 + 2, rows2, y3, lambda i, j: ((gy * y2 - 8 + i) >> 1) == j)
+    twice_y1 = blocks(b2 + 2, rows1, rows2, lambda i, j: (i >> 1) + 4 == j)
+    upper = lax.broadcasted_iota(jnp.int32, (8, lanes), 0) < 4
+
+    def pairs(value):
+        n = value.shape[0]
+        tmp[0:n] = value
+        return tmp[pl.ds(0, n // 2, 2)] + tmp[pl.ds(1, n // 2, 2)]
 
     fine = cheb_steps(FINE_DEGREE, LOW_FINE, HIGH_BOUND)
     coarse = cheb_steps(COARSE_DEGREE, LOW_COARSE, HIGH_BOUND)
@@ -278,17 +297,19 @@
                 pl.when(valid(dx, dy))(copy.wait_send)
 
         start(copies1)
-        for q in range(q0, q0 + count):
-            for p in range(b2):
-                both = f1[q, H1 + 2 * p, 8 : 8 + by] + f1[q, H1 + 2 * p + 1, 8 : 8 + by]
-                f2[q, 2 * b2 + p, 8 : 8 + y2] = dot(half_y_mat, dot(both, half_z_mat))
+        parts = [
+            f1[q, H1 + 2 * p, 8 : 8 + by] + f1[q, H1 + 2 * p + 1, 8 : 8 + by]
+            for q in range(q0, q0 + count) for p in range(b2)
+        ]
+        halves = pairs(dot(jnp.concatenate(parts, axis=0), half_z_mat))
+        parts = [halves[k * y2 : (k + 1) * y2] for k in range(count * b2)]
+        for k in range(count * b2):
+            f2[q0 + k // b2, 2 * b2 + k % b2, 8 : 8 + y2] = parts[k]
         start(copies2)
-        for q in range(q0, q0 + count):
-            tile = jnp.zeros((8, lanes), F32)
-            for r in range(bx // 4):
-                both = f2[q, 2 * b2 + 2 * r, 8 : 8 + y2] + f2[q, 2 * b2 + 2 * r + 1, 8 : 8 + y2]
-                tile = tile + dot(quarter_y[r], dot(both, half_z2))
-            gath[q, xi, gy] = tile
+        parts = [parts[2 * k] + parts[2 * k + 1] for k in range(count * b3)]
+        halves = pairs(dot(jnp.concatenate(parts, axis=0), half_z2))
+        for k in range(count):
+            gath[q0 + k, xi, gy] = halves[k * 8 : (k + 1) * 8]
 
         def along_y(o):
             return remote(
@@ -339,17 +360,19 @@
             slot = 0 if q == 0 else 1
 
             def unpack(x, q=q, slot=slot):
-                tiles = gath[q, x].reshape(gy_size * 8, lanes)
-                for r in range(bx // 4):
-                    f3[slot, 1 + x * (bx // 4) + r] = dot(spread[r], tiles)
+                for k in range(gy_size // 2):
+                    even, odd = gath[q, x, 2 * k], gath[q, x, 2 * k + 1]
+                    place = slice(8 * k, 8 * k + 8)
+                    f3[slot, 1 + 2 * x, place] = jnp.where(upper, even, pltpu.roll(odd, 4, 0))
+                    f3[slot, 2 + 2 * x, place] = jnp.where(upper, pltpu.roll(even, 4, 0), odd)
 
             loop(0, nx, unpack, 4)
 
-            def shrink(x, slot=slot):
-                both = f3[slot, 1 + 2 * x] + f3[slot, 2 + 2 * x]
-                f4[slot, 1 + x] = dot(half_y3, dot(both, half_z2))
-
-            loop(0, n4, shrink, 4)
+        slots = (0, 1) if count == 2 else (1,)
+        parts = [f3[slot, 1 + 2 * x] + f3[slot, 2 + 2 * x] for slot in slots for x in range(n4)]
+        halves = pairs(dot(jnp.concatenate(parts, axis=0), half_z2))
+        for k in range(count * n4):
+            f4[slots[k // n4], 1 + k % n4] = halves[k * y4 : (k + 1) * y4]
         if outer == 0:
             build(f3.at[0], w3, inv3, 1, n3 + 1, 4)
             build(f4.at[0], w4, inv4, 1, n4 + 1, 4)
@@ -365,19 +388,24 @@
         for k in range(FINE_DEGREE - 1):
             advance(w3, t3, d3.at[k], d3.at[k + 1], fine[1][k], fine[2][k], 1, n3 + 1, 4)
 
-        def combine3(x):
-            wide = dot(twice_y3, dot(c4[1 + x], twice_z))
+        wide = dot(jnp.concatenate([c4[1 + x] for x in range(n4)], axis=0), twice_z)
+        tmp[pl.ds(0, n4 * y4, 2)] = wide
+        tmp[pl.ds(1, n4 * y4, 2)] = wide
+        for x in range(n4):
+            add = tmp[x * y3 : (x + 1) * y3]
             for p in (1 + 2 * x, 2 + 2 * x):
-                c3[p] = ((d3[0, p] + d3[1, p]) + (d3[2, p] + d3[3, p])) + d3[4, p] + wide
-
-        loop(0, n4, combine3, 4)
-        b3 = b2 // 2
+                c3[p] = ((d3[0, p] + d3[1, p]) + (d3[2, p] + d3[3, p])) + d3[4, p] + add
+        parts = [c3[jnp.clip(xi * b3 + r, 0, n3 - 1) + 1] for r in range(-1, b3 + 1)]
+        wide = dot(twice_y2, dot(jnp.concatenate(parts, axis=0), twice_z))
         for r in range(-1, b3 + 1):
-            plane = jnp.clip(xi * b3 + r, 0, n3 - 1) + 1
-            wide = dot(twice_y2, dot(c3[plane], twice_z))
+            add = wide[(r + 1) * rows2 : (r + 2) * rows2]
             for p in (2 * b2 + 2 * r, 2 * b2 + 2 * r + 1):
                 if 2 * b2 - 1 <= p < 3 * b2 + 1:
-                    c2[p] = ((d2[0, p] + d2[1, p]) + (d2[2, p] + d2[3, p])) + d2[4, p] + wide
+                    c2[p] = ((d2[0, p] + d2[1, p]) + (d2[2, p] + d2[3, p])) + d2[4, p] + add
+        parts = [c2[2 * b2 + r] for r in range(-1, b2 + 1)]
+        wide1 = dot(twice_y1, dot(jnp.concatenate(parts, axis=0), twice_z1))
+        for r in range(b2 + 2):
+            c1[r] = wide1[r * rows1 : (r + 1) * rows1]
 
         finish(copies1)
         low, high = H1 - 5, H1 + bx + 5
@@ -388,15 +416,11 @@
             low, high = low + 1, high - 1
             advance(w1, t1, d1.at[k], d1.at[k + 1], fine[1][k], fine[2][k], low, high, 2)
 
-        def combine1(r):
-            wide = dot(twice_y1, dot(c2[2 * b2 + r], twice_z1))
-            return wide
-
         for r in range(-1, b2 + 1):
-            wide = combine1(r)
+            add = c1[r + 1]
             for p in (H1 + 2 * r, H1 + 2 * r + 1):
                 if H1 - 1 <= p < H1 + bx + 1:
-                    both = ((d1[0, p] + d1[1, p]) + (d1[2, p] + d1[3, p])) + d1[4, p] + wide
+                    both = ((d1[0, p] + d1[1, p]) + (d1[2, p] + d1[3, p])) + d1[4, p] + add
                     if outer == 0:
                         u1[p] = DAMPING * both
                     else:
@@ -450,7 +474,7 @@
         return pl.pallas_call(
             functools.partial(kernel, gx_size, gy_size),
             out_shape=(jax.ShapeDtypeStruct(right_side.shape, F32),) * 2,
-            in_specs=[pl.BlockSpec(memory_space=pltpu.VMEM)] * 2,
+            in_specs=[pl.BlockSpec(memory_space=pltpu.HBM)] * 2,
             out_specs=(pl.BlockSpec(memory_space=pltpu.VMEM),) * 2,
             scratch_shapes=[
                 vm(3, p1, r1, l1), vm(6, p1, r1, l1), vm(p1, r1, l1), vm(p1, r1, l1), vm(p1, r1, l1),
@@ -462,11 +486,12 @@
                 vm(FINE_DEGREE, p3, r3, lanes), vm(p3, r3, lanes),
                 vm(2, p4, r4, lanes), vm(6, p4, r4, lanes), vm(p4, r4, lanes), vm(p4, r4, lanes),
                 vm(2, p4, r4, lanes), vm(p4, r4, lanes),
+                vm(max((p3 - 2) * r3, 2 * b2 * by), lanes), vm(b2 + 2, r1, l1), sem(2),
                 sem(2), sem(2), sem(2, 8), sem(2, 8), sem(2, 14), sem(2, 14),
                 sem(2, gy_size), sem(2, gy_size), sem(2, nx), sem(2, nx), sem(2), sem(2),
             ],
             compiler_params=pltpu.CompilerParams(
-                collective_id=0, has_side_effects=True, vmem_limit_bytes=48 * 1024 * 1024
+                collective_id=0, has_side_effects=True, vmem_limit_bytes=64 * 1024 * 1024
             ),
         )(right_side, coefficient)
 

time: 76.3 us -> 63 us (0.83)
  Pallas kernels: 72.4 us -> 59.9 us
  local copies, waits for them, and re-layouts: 3.11 us -> 2.26 us
    pallas_call x1, Pallas kernels: 72.4 us -> 59.9 us  [on_device(): pl.pallas_call(functools.partial(kernel, gx_size, gy_size), out_shape=(ja...]
    unnamed x6 -> x4, local copies, waits for them, and re-layouts: 3.11 us -> 2.26 us
where the time goes in v2:
time: 63 us; the launch traced here: 62.8 us
  Pallas kernels  59.9 us (95%)
  local copies, waits for them, and re-layouts  2.26 us (4%)
  between operations  0.65 us (1%)
    pallas_call x1, Pallas kernels, on_device(): pl.pallas_call(functools.partial(kernel, gx_size, gy_size), out_shape=(ja...  59.9 us
    unnamed x4, local copies, waits for them, and re-layouts  2.26 us

profile of v2, /device:TPU:0, one launch (start us, length us, event | category | flops | bytes accessed | tf_op | source)
XLA Modules:
  0.0 62.8 jit_solution(3458938104511573613)
XLA Ops:
  0.6 59.9 %shard_map.41 = (f32[16,16,128]{2,1,0:T(8,128)}, f32[16,16,128]{2,1,0:T(8,128)}) custom-call(f32[16,16,128]{2,1,0:T(8,128)} %rhs_ref.1, f32[16,16,128]{2,1,0:T(8,128)} %coef_ref.1), custom_call_target="tpu_custom_call" | custom-call | tf_op jit(solution)/shard_map/pallas_call | solution.py:474
  60.6 0.0 copy-start
  60.6 1.6 %copy.6 = f32[16,16,128]{2,1,0:T(8,128)} copy(f32[16,16,128]{2,1,0:T(8,128)} %get-tuple-element.4) | data formatting | bytes 262144
  62.2 0.0 copy-done
  62.2 0.7 %copy.7 = f32[16,16,128]{2,1,0:T(8,128)} copy(f32[16,16,128]{2,1,0:T(8,128)S(1)} %copy-done) | data formatting | bytes 262144
Async XLA Ops:
  60.6 1.6 %copy-start = (f32[16,16,128]{2,1,0:T(8,128)S(1)}, f32[16,16,128]{2,1,0:T(8,128)}, u32[]{:S(2)}) copy-start(f32[16,16,128]{2,1,0:T(8,128)} %get-tuple-element.5) | copy-start | bytes 393220

commit v3 on v2

--- a/solution.py
+++ b/solution.py
@@ -262,10 +262,11 @@
 
         copies1 = []
         for k, (dx, dy) in enumerate(close):
+            h = H1 - outer - (1 if dy else 0)
             src_x, dst_x = {
                 0: (own_x, own_x),
-                1: (pl.ds(bx, H1), pl.ds(0, H1)),
-                -1: (pl.ds(H1, H1), pl.ds(H1 + bx, H1)),
+                1: (pl.ds(H1 + bx - h, h), pl.ds(H1 - h, h)),
+                -1: (pl.ds(H1, h), pl.ds(H1 + bx, h)),
             }[dx]
             src_y, dst_y = {
                 0: (own_y, own_y),
@@ -278,6 +279,8 @@
             )))
         copies2 = []
         for k, (dx, dy) in enumerate(around):
+            if outer and abs(dx) == 2 and dy:
+                continue
             copies2.append((dx, dy, remote(
                 f2.at[qs, pl.ds(2 * b2, b2), pl.ds(8, y2)],
                 f2.at[qs, pl.ds(2 * b2 - b2 * dx, b2), pl.ds(8 - y2 * dy, y2)],
@@ -296,7 +299,6 @@
             for dx, dy, copy in copies:
                 pl.when(valid(dx, dy))(copy.wait_send)
 
-        start(copies1)
         parts = [
             f1[q, H1 + 2 * p, 8 : 8 + by] + f1[q, H1 + 2 * p + 1, 8 : 8 + by]
             for q in range(q0, q0 + count) for p in range(b2)
@@ -344,15 +346,8 @@
         for o in range(1, nx):
             along_x(o).start()
 
+        start(copies1)
         finish(copies2)
-        low, high = 2 * b2 - 5, 3 * b2 + 5
-        if outer == 0:
-            build(f2.at[0], w2, inv2, low, high, 2)
-        first_update(f2.at[now], inv2, t2, d2.at[0], 0.25, fine[0], low, high, 7)
-        for k in range(FINE_DEGREE - 1):
-            low, high = low + 1, high - 1
-            advance(w2, t2, d2.at[k], d2.at[k + 1], fine[1][k], fine[2][k], low, high, 4)
-        low2 = low
 
         for o in range(1, nx):
             from_x(o).wait_recv()
@@ -373,20 +368,50 @@
         halves = pairs(dot(jnp.concatenate(parts, axis=0), half_z2))
         for k in range(count * n4):
             f4[slots[k // n4], 1 + k % n4] = halves[k * y4 : (k + 1) * y4]
+        low, high = 2 * b2 - 5, 3 * b2 + 5
         if outer == 0:
+            build(f4.at[0], w4, inv4, 1, n4 + 1, 8)
             build(f3.at[0], w3, inv3, 1, n3 + 1, 4)
-            build(f4.at[0], w4, inv4, 1, n4 + 1, 4)
+            build(f2.at[0], w2, inv2, low, high, 4)
+        small = n4 * y4 <= 64
+        width = 16 if small else 4
         first_update(f4.at[1], inv4, t4, d4.at[0], 0.015625, coarse[0], 1, n4 + 1, 8)
-
-        def begin4(p):
-            c4[p] = d4[0, p]
-
-        loop(1, n4 + 1, begin4, 8)
+        first_update(f3.at[1], inv3, t3, d3.at[0], 0.0625, fine[0], 1, n3 + 1, width)
+        first_update(f2.at[now], inv2, t2, d2.at[0], 0.25, fine[0], low, high, 16)
+        if small:
+            zero = jnp.zeros((y4, lanes), F32)
+            vs = [d4[0, 1 + p] for p in range(n4)]
+            ts = [t4[1 + p] for p in range(n4)]
+            sums = list(vs)
+        else:
+
+            def begin4(p):
+                c4[p] = d4[0, p]
+
+            loop(1, n4 + 1, begin4, 8)
         for k in range(COARSE_DEGREE - 1):
-            advance(w4, t4, d4.at[k % 2], d4.at[(k + 1) % 2], coarse[1][k], coarse[2][k], 1, n4 + 1, 8, c4)
-        first_update(f3.at[1], inv3, t3, d3.at[0], 0.0625, fine[0], 1, n3 + 1, 8)
-        for k in range(FINE_DEGREE - 1):
-            advance(w3, t3, d3.at[k], d3.at[k + 1], fine[1][k], fine[2][k], 1, n3 + 1, 4)
+            if small:
+                edged = [zero] + vs + [zero]
+                news = []
+                for p in range(n4):
+                    c = vs[p]
+                    acc = w4[0, 1 + p] * edged[p] + w4[1, 1 + p] * edged[p + 2]
+                    acc2 = w4[2, 1 + p] * pltpu.roll(c, 1, 0) + w4[3, 1 + p] * pltpu.roll(c, y4 - 1, 0)
+                    acc3 = w4[4, 1 + p] * pltpu.roll(c, 1, 1) + w4[5, 1 + p] * pltpu.roll(c, lanes - 1, 1)
+                    ts[p] = ts[p] - c + (acc + (acc2 + acc3))
+                    news.append(coarse[1][k] * c + coarse[2][k] * ts[p])
+                    sums[p] = sums[p] + news[p]
+                vs = news
+            else:
+                advance(w4, t4, d4.at[k % 2], d4.at[(k + 1) % 2], coarse[1][k], coarse[2][k], 1, n4 + 1, 8, c4)
+            if k % 3 == 0 and k // 3 < FINE_DEGREE - 1:
+                m = k // 3
+                advance(w3, t3, d3.at[m], d3.at[m + 1], fine[1][m], fine[2][m], 1, n3 + 1, width)
+                low, high = low + 1, high - 1
+                advance(w2, t2, d2.at[m], d2.at[m + 1], fine[1][m], fine[2][m], low, high, 16)
+        if small:
+            for p in range(n4):
+                c4[1 + p] = sums[p]
 
         wide = dot(jnp.concatenate([c4[1 + x] for x in range(n4)], axis=0), twice_z)
         tmp[pl.ds(0, n4 * y4, 2)] = wide
@@ -414,7 +439,7 @@
         first_update(f1.at[now], inv1, t1, d1.at[0], 1.0, fine[0], low, high, 2)
         for k in range(FINE_DEGREE - 1):
             low, high = low + 1, high - 1
-            advance(w1, t1, d1.at[k], d1.at[k + 1], fine[1][k], fine[2][k], low, high, 2)
+            advance(w1, t1, d1.at[k], d1.at[k + 1], fine[1][k], fine[2][k], low, high, 4)
 
         for r in range(-1, b2 + 1):
             add = c1[r + 1]

time: 63 us -> 51.8 us (0.82)
  Pallas kernels: 59.9 us -> 48.7 us
    pallas_call x1, Pallas kernels: 59.9 us -> 48.7 us  [on_device(): pl.pallas_call(functools.partial(kernel, gx_size, gy_size), out_shape=(ja...]
where the time goes in v3:
time: 51.8 us; the launch traced here: 51.6 us
  Pallas kernels  48.7 us (94%)
  local copies, waits for them, and re-layouts  2.26 us (4%)
  between operations  0.65 us (1%)
    pallas_call x1, Pallas kernels, on_device(): pl.pallas_call(functools.partial(kernel, gx_size, gy_size), out_shape=(ja...  48.7 us
    unnamed x4, local copies, waits for them, and re-layouts  2.26 us

profile of v3, /device:TPU:0, one launch (start us, length us, event | category | flops | bytes accessed | tf_op | source)
XLA Modules:
  0.0 51.6 jit_solution(621134421877830680)
XLA Ops:
  0.6 48.7 %shard_map.41 = (f32[16,16,128]{2,1,0:T(8,128)}, f32[16,16,128]{2,1,0:T(8,128)}) custom-call(f32[16,16,128]{2,1,0:T(8,128)} %rhs_ref.1, f32[16,16,128]{2,1,0:T(8,128)} %coef_ref.1), custom_call_target="tpu_custom_call" | custom-call | tf_op jit(solution)/shard_map/pallas_call | solution.py:499
  49.4 0.0 copy-start
  49.4 1.6 %copy.6 = f32[16,16,128]{2,1,0:T(8,128)} copy(f32[16,16,128]{2,1,0:T(8,128)} %get-tuple-element.4) | data formatting | bytes 262144
  51.0 0.0 copy-done
  51.0 0.7 %copy.7 = f32[16,16,128]{2,1,0:T(8,128)} copy(f32[16,16,128]{2,1,0:T(8,128)S(1)} %copy-done) | data formatting | bytes 262144
Async XLA Ops:
  49.4 1.6 %copy-start = (f32[16,16,128]{2,1,0:T(8,128)S(1)}, f32[16,16,128]{2,1,0:T(8,128)}, u32[]{:S(2)}) copy-start(f32[16,16,128]{2,1,0:T(8,128)} %get-tuple-element.5) | copy-start | bytes 393220

commit v4 on v3

--- a/solution.py
+++ b/solution.py
@@ -35,7 +35,21 @@
 
 
 def dot(a, b):
-    return jnp.dot(a, b, precision=lax.Precision.HIGHEST, preferred_element_type=F32)
+    def times(x, y):
+        return jnp.dot(x, y, preferred_element_type=F32)
+
+    if a.dtype == jnp.bfloat16:
+        top, middle, rest = thirds(b)
+        return times(a, top) + (times(a, middle) + times(a, rest))
+    top, middle, rest = thirds(a)
+    return times(top, b) + (times(middle, b) + times(rest, b))
+
+
+def thirds(x):
+    top = x.astype(jnp.bfloat16)
+    left = x - top.astype(F32)
+    middle = left.astype(jnp.bfloat16)
+    return top, middle, (left - middle.astype(F32)).astype(jnp.bfloat16)
 
 
 def loop(low, high, body, unroll):
@@ -57,7 +71,7 @@
 def pick(rows, columns, rule, value=1.0):
     i = lax.broadcasted_iota(jnp.int32, (rows, columns), 0)
     j = lax.broadcasted_iota(jnp.int32, (rows, columns), 1)
-    return jnp.where(rule(i, j), value, 0.0).astype(F32)
+    return jnp.where(rule(i, j), value, 0.0).astype(jnp.bfloat16)
 
 
 def build(a, w, inv, low, high, unroll, diag=None):
@@ -245,6 +259,7 @@
 
     twice_y2 = blocks(b3 + 2, rows2, y3, lambda i, j: ((gy * y2 - 8 + i) >> 1) == j)
     twice_y1 = blocks(b2 + 2, rows1, rows2, lambda i, j: (i >> 1) + 4 == j)
+    first_half = lax.broadcasted_iota(jnp.int32, (8, lanes), 1) < lanes // 2
     upper = lax.broadcasted_iota(jnp.int32, (8, lanes), 0) < 4
 
     def pairs(value):
@@ -310,32 +325,34 @@
         start(copies2)
         parts = [parts[2 * k] + parts[2 * k + 1] for k in range(count * b3)]
         halves = pairs(dot(jnp.concatenate(parts, axis=0), half_z2))
-        for k in range(count):
-            gath[q0 + k, xi, gy] = halves[k * 8 : (k + 1) * 8]
+        if count == 2:
+            gath[outer, xi, gy] = halves[0:8] + pltpu.roll(halves[8:16], lanes // 2, 1)
+        else:
+            gath[outer, xi, gy] = halves
 
         def along_y(o):
             return remote(
-                gath.at[qs, xi, gy], gath.at[qs, xi, gy],
+                gath.at[outer, xi, gy], gath.at[outer, xi, gy],
                 gy_send.at[outer, o], gy_recv.at[outer, o], xi, lax.rem(gy + o, gy_size),
             )
 
         def from_y(o):
             y = lax.rem(gy + gy_size - o, gy_size)
             return remote(
-                gath.at[qs, xi, y], gath.at[qs, xi, y],
+                gath.at[outer, xi, y], gath.at[outer, xi, y],
                 gy_send.at[outer, o], gy_recv.at[outer, o], xi, lax.rem(gy + o, gy_size),
             )
 
         def along_x(o):
             return remote(
-                gath.at[qs, xi], gath.at[qs, xi],
+                gath.at[outer, xi], gath.at[outer, xi],
                 gx_send.at[outer, o], gx_recv.at[outer, o], lax.rem(xi + o, nx), gy,
             )
 
         def from_x(o):
             x = lax.rem(xi + nx - o, nx)
             return remote(
-                gath.at[qs, x], gath.at[qs, x],
+                gath.at[outer, x], gath.at[outer, x],
                 gx_send.at[outer, o], gx_recv.at[outer, o], lax.rem(xi + o, nx), gy,
             )
 
@@ -348,36 +365,42 @@
 
         start(copies1)
         finish(copies2)
+        low, high = 2 * b2 - 5, 3 * b2 + 5
+        if outer == 0:
+            build(f2.at[0], w2, inv2, low, high, 4)
+        first_update(f2.at[now], inv2, t2, d2.at[0], 0.25, fine[0], low, high, 16)
+        for k in range(FINE_DEGREE - 1):
+            low, high = low + 1, high - 1
+            advance(w2, t2, d2.at[k], d2.at[k + 1], fine[1][k], fine[2][k], low, high, 16)
 
         for o in range(1, nx):
             from_x(o).wait_recv()
-        for q in range(q0, q0 + count):
-            slot = 0 if q == 0 else 1
-
-            def unpack(x, q=q, slot=slot):
-                for k in range(gy_size // 2):
-                    even, odd = gath[q, x, 2 * k], gath[q, x, 2 * k + 1]
-                    place = slice(8 * k, 8 * k + 8)
-                    f3[slot, 1 + 2 * x, place] = jnp.where(upper, even, pltpu.roll(odd, 4, 0))
-                    f3[slot, 2 + 2 * x, place] = jnp.where(upper, pltpu.roll(even, 4, 0), odd)
-
-            loop(0, nx, unpack, 4)
+        def unpack(x):
+            for k in range(gy_size // 2):
+                even, odd = gath[outer, x, 2 * k], gath[outer, x, 2 * k + 1]
+                place = slice(8 * k, 8 * k + 8)
+                one = jnp.where(upper, even, pltpu.roll(odd, 4, 0))
+                two = jnp.where(upper, pltpu.roll(even, 4, 0), odd)
+                for p, value in ((1 + 2 * x, one), (2 + 2 * x, two)):
+                    if count == 2:
+                        f3[0, p, place] = jnp.where(first_half, value, 0.0)
+                        value = jnp.where(first_half, pltpu.roll(value, lanes // 2, 1), 0.0)
+                    f3[1, p, place] = value
+
+        loop(0, nx, unpack, 8)
 
         slots = (0, 1) if count == 2 else (1,)
         parts = [f3[slot, 1 + 2 * x] + f3[slot, 2 + 2 * x] for slot in slots for x in range(n4)]
         halves = pairs(dot(jnp.concatenate(parts, axis=0), half_z2))
         for k in range(count * n4):
             f4[slots[k // n4], 1 + k % n4] = halves[k * y4 : (k + 1) * y4]
-        low, high = 2 * b2 - 5, 3 * b2 + 5
         if outer == 0:
             build(f4.at[0], w4, inv4, 1, n4 + 1, 8)
             build(f3.at[0], w3, inv3, 1, n3 + 1, 4)
-            build(f2.at[0], w2, inv2, low, high, 4)
         small = n4 * y4 <= 64
         width = 16 if small else 4
         first_update(f4.at[1], inv4, t4, d4.at[0], 0.015625, coarse[0], 1, n4 + 1, 8)
         first_update(f3.at[1], inv3, t3, d3.at[0], 0.0625, fine[0], 1, n3 + 1, width)
-        first_update(f2.at[now], inv2, t2, d2.at[0], 0.25, fine[0], low, high, 16)
         if small:
             zero = jnp.zeros((y4, lanes), F32)
             vs = [d4[0, 1 + p] for p in range(n4)]
@@ -407,8 +430,6 @@
             if k % 3 == 0 and k // 3 < FINE_DEGREE - 1:
                 m = k // 3
                 advance(w3, t3, d3.at[m], d3.at[m + 1], fine[1][m], fine[2][m], 1, n3 + 1, width)
-                low, high = low + 1, high - 1
-                advance(w2, t2, d2.at[m], d2.at[m + 1], fine[1][m], fine[2][m], low, high, 16)
         if small:
             for p in range(n4):
                 c4[1 + p] = sums[p]
@@ -506,7 +527,7 @@
                 vm(FINE_DEGREE, p1, r1, l1), vm(p1, r1, l1), vm(bx, by, l1),
                 vm(3, p2, r2, lanes), vm(6, p2, r2, lanes), vm(p2, r2, lanes), vm(p2, r2, lanes),
                 vm(FINE_DEGREE, p2, r2, lanes), vm(p2, r2, lanes),
-                vm(3, nx, gy_size, 8, lanes),
+                vm(2, nx, gy_size, 8, lanes),
                 vm(2, p3, r3, lanes), vm(6, p3, r3, lanes), vm(p3, r3, lanes), vm(p3, r3, lanes),
                 vm(FINE_DEGREE, p3, r3, lanes), vm(p3, r3, lanes),
                 vm(2, p4, r4, lanes), vm(6, p4, r4, lanes), vm(p4, r4, lanes), vm(p4, r4, lanes),

time: 51.8 us -> 47.6 us (0.919)
  Pallas kernels: 48.7 us -> 44.5 us
    pallas_call x1, Pallas kernels: 48.7 us -> 44.5 us  [on_device(): pl.pallas_call(functools.partial(kernel, gx_size, gy_size), out_shape=(ja...]
where the time goes in v4:
time: 47.6 us; the launch traced here: 47.4 us
  Pallas kernels  44.5 us (93%)
  local copies, waits for them, and re-layouts  2.26 us (5%)
  between operations  0.65 us (1%)
    pallas_call x1, Pallas kernels, on_device(): pl.pallas_call(functools.partial(kernel, gx_size, gy_size), out_shape=(ja...  44.5 us
    unnamed x4, local copies, waits for them, and re-layouts  2.26 us

profile of v4, /device:TPU:0, one launch (start us, length us, event | category | flops | bytes accessed | tf_op | source)
XLA Modules:
  0.0 47.4 jit_solution(9629229515506872166)
XLA Ops:
  0.6 44.5 %shard_map.41 = (f32[16,16,128]{2,1,0:T(8,128)}, f32[16,16,128]{2,1,0:T(8,128)}) custom-call(f32[16,16,128]{2,1,0:T(8,128)} %rhs_ref.1, f32[16,16,128]{2,1,0:T(8,128)} %coef_ref.1), custom_call_target="tpu_custom_call" | custom-call | tf_op jit(solution)/shard_map/pallas_call | solution.py:520
  45.2 0.0 copy-start
  45.2 1.6 %copy.6 = f32[16,16,128]{2,1,0:T(8,128)} copy(f32[16,16,128]{2,1,0:T(8,128)} %get-tuple-element.4) | data formatting | bytes 262144
  46.8 0.0 copy-done
  46.8 0.7 %copy.7 = f32[16,16,128]{2,1,0:T(8,128)} copy(f32[16,16,128]{2,1,0:T(8,128)S(1)} %copy-done) | data formatting | bytes 262144
Async XLA Ops:
  45.2 1.6 %copy-start = (f32[16,16,128]{2,1,0:T(8,128)S(1)}, f32[16,16,128]{2,1,0:T(8,128)}, u32[]{:S(2)}) copy-start(f32[16,16,128]{2,1,0:T(8,128)} %get-tuple-element.5) | copy-start | bytes 393220

commit v5 on v4

--- a/solution.py
+++ b/solution.py
@@ -456,11 +456,11 @@
         finish(copies1)
         low, high = H1 - 5, H1 + bx + 5
         if outer == 0:
-            build(f1.at[0], w1, inv1, low, high, 1, diag1)
-        first_update(f1.at[now], inv1, t1, d1.at[0], 1.0, fine[0], low, high, 2)
+            build(f1.at[0], w1, inv1, low, high, 3, diag1)
+        first_update(f1.at[now], inv1, t1, d1.at[0], 1.0, fine[0], low, high, 6)
         for k in range(FINE_DEGREE - 1):
             low, high = low + 1, high - 1
-            advance(w1, t1, d1.at[k], d1.at[k + 1], fine[1][k], fine[2][k], low, high, 4)
+            advance(w1, t1, d1.at[k], d1.at[k + 1], fine[1][k], fine[2][k], low, high, (high - low) // 2)
 
         for r in range(-1, b2 + 1):
             add = c1[r + 1]
@@ -480,7 +480,7 @@
             else:
                 last[p - H1] = value[8 : 8 + by]
 
-        loop(H1, H1 + bx, leftover, 2)
+        loop(H1, H1 + bx, leftover, 4)
         drain(copies1)
         drain(copies2)
         for o in range(1, gy_size):

time: 47.6 us -> 45.9 us (0.964)
  Pallas kernels: 44.5 us -> 42.8 us
    pallas_call x1, Pallas kernels: 44.5 us -> 42.8 us  [on_device(): pl.pallas_call(functools.partial(kernel, gx_size, gy_size), out_shape=(ja...]
where the time goes in v5:
time: 45.9 us; the launch traced here: 45.7 us
  Pallas kernels  42.8 us (93%)
  local copies, waits for them, and re-layouts  2.26 us (5%)
  between operations  0.65 us (1%)
    pallas_call x1, Pallas kernels, on_device(): pl.pallas_call(functools.partial(kernel, gx_size, gy_size), out_shape=(ja...  42.8 us
    unnamed x4, local copies, waits for them, and re-layouts  2.26 us

profile of v5, /device:TPU:0, one launch (start us, length us, event | category | flops | bytes accessed | tf_op | source)
XLA Modules:
  0.0 45.7 jit_solution(11055094251246050332)
XLA Ops:
  0.6 42.8 %shard_map.41 = (f32[16,16,128]{2,1,0:T(8,128)}, f32[16,16,128]{2,1,0:T(8,128)}) custom-call(f32[16,16,128]{2,1,0:T(8,128)} %rhs_ref.1, f32[16,16,128]{2,1,0:T(8,128)} %coef_ref.1), custom_call_target="tpu_custom_call" | custom-call | tf_op jit(solution)/shard_map/pallas_call | solution.py:520
  43.5 0.0 copy-start
  43.5 1.6 %copy.6 = f32[16,16,128]{2,1,0:T(8,128)} copy(f32[16,16,128]{2,1,0:T(8,128)} %get-tuple-element.4) | data formatting | bytes 262144
  45.1 0.0 copy-done
  45.1 0.7 %copy.7 = f32[16,16,128]{2,1,0:T(8,128)} copy(f32[16,16,128]{2,1,0:T(8,128)S(1)} %copy-done) | data formatting | bytes 262144
Async XLA Ops:
  43.5 1.6 %copy-start = (f32[16,16,128]{2,1,0:T(8,128)S(1)}, f32[16,16,128]{2,1,0:T(8,128)}, u32[]{:S(2)}) copy-start(f32[16,16,128]{2,1,0:T(8,128)} %get-tuple-element.5) | copy-start | bytes 393220
